TPU v7x, 32 devices: a whole 2x2x4 slice. The times are simulated.
32 devices in a mesh: section: 4 (over y, x), expert: 8 (over z, core).
Axes of the slice: x: 2, y: 2, z: 4, core: 2. Of those that a mesh axis runs over, the one named last changes fastest.
Arguments:
- hidden_in: bfloat16 [4, 1024, 2880], P('section', 'expert')
- norm_gain: float32 [4, 2880], P('section'), may hold values from 0.25 to 1.75
- out_grad: bfloat16 [4, 1024, 2880], P('section', 'expert'), may hold values from -6 to 6
- expert_ids: int32 [4, 1024, 4], P('section', 'expert'), may hold values from 0 to 7, all different within a row; in each aligned block of 128 rows (0 to 127, 128 to 255, ..., all dimensions but the last counted through in order) at most 80 rows name the same one
- route_weights: float32 [4, 1024, 4], P('section', 'expert'), may hold values from 0 to 1, as said below
- w_gate_up: bfloat16 [4, 8, 2880, 2880], P('section', 'expert'), may hold values from -0.109375 to 0.109375
- w_down: bfloat16 [4, 8, 1440, 2880], P('section', 'expert'), may hold values from -0.15625 to 0.15625
Outputs:
- input_grad: bfloat16 [4, 1024, 2880], P('section', 'expert')
Inputs may be any that keep to these rules, and one draw needn't show every extreme that they name: `expert_ids`: each token names 4 different experts. The 128 tokens of one index of expert in one section name any one expert at most 80 times, a bound that some block reaches. `route_weights`: each token's 4 weights are positive and sum to one.
All inputs are finite; a program needn't handle non-finite values.
Results may differ from a plain program's by a relative error of at most 0.0047.
Values may be sent and summed in bfloat16 or wider, within the bound.
A program may use at most 128 MiB of HBM per device.

v0:
```python
import jax
import jax.numpy as jnp
from jax import lax
from jax.sharding import PartitionSpec as P

glu_alpha = 1.702
norm_eps = 1e-05


def shifted(value, axis, steps):
    count = lax.axis_size(axis)
    pairs = [(source, (source + steps) % count) for source in range(count)]
    return lax.ppermute(value, axis, pairs)


def expert_backward(rows_in, grad_rows, gate_up, down_proj):
    preact = jnp.dot(rows_in, gate_up, preferred_element_type=jnp.float32)
    dact = lax.dot_general(
        grad_rows, down_proj, (((1,), (1,)), ((), ())), preferred_element_type=jnp.float32
    )
    half = down_proj.shape[0]
    gate = preact[:, :half]
    up_part = preact[:, half:]
    sig = jax.nn.sigmoid(glu_alpha * gate)
    dgate = dact * (up_part + 1.0) * (sig + glu_alpha * gate * sig * (1.0 - sig))
    dup = dact * gate * sig
    dpre = jnp.concatenate([dgate, dup], axis=1).astype(jnp.bfloat16)
    result = lax.dot_general(
        dpre, gate_up, (((1,), (1,)), ((), ())), preferred_element_type=jnp.float32
    )
    return result.astype(jnp.bfloat16)


def slab_backward(inputs_slab, grads_slab, gate_up, down_proj):
    sources, slot_count, feat_width = inputs_slab.shape
    flat_out = expert_backward(
        inputs_slab.reshape(sources * slot_count, feat_width),
        grads_slab.reshape(sources * slot_count, feat_width),
        gate_up,
        down_proj,
    )
    return flat_out.reshape(sources, slot_count, feat_width)


def send_back(slab):
    return lax.all_to_all(slab, "expert", split_axis=0, concat_axis=0, tiled=True)


def per_device(hidden_in, norm_gain, out_grad, expert_ids, route_weights, w_gate_up, w_down):
    tokens = hidden_in[0]
    gain_vector_row = norm_gain[0]
    incoming_gradient = out_grad[0]
    routes = expert_ids[0]
    weights = route_weights[0]
    gate_up = w_gate_up[0, 0]
    down_proj = w_down[0, 0]
    tok_count = tokens.shape[0]
    feat_width = tokens.shape[1]
    top_count = routes.shape[1]
    experts = lax.axis_size("expert")
    capacity = max(2, tok_count * top_count * 5 // (4 * experts))
    input_single_precision = tokens.astype(jnp.float32)
    inverse_root_mean = lax.rsqrt(
        jnp.mean(input_single_precision * input_single_precision, axis=-1, keepdims=True) + norm_eps
    )
    normalized_input = input_single_precision * inverse_root_mean
    rescaled_input = (normalized_input * gain_vector_row[None, :]).astype(jnp.bfloat16)
    flat_ids = routes.reshape(-1)
    assign = flat_ids.shape[0]
    one_hot = (flat_ids[:, None] == jnp.arange(experts, dtype=jnp.int32)[None, :]).astype(jnp.int32)
    slot_rank = jnp.sum((jnp.cumsum(one_hot, axis=0) - one_hot) * one_hot, axis=1)
    slot_index = flat_ids * capacity + slot_rank
    source_of = (
        jnp.full((experts * capacity,), assign, jnp.int32)
        .at[slot_index]
        .set(jnp.arange(assign, dtype=jnp.int32))
    )
    token_of = source_of // top_count
    normed_pad = jnp.concatenate([rescaled_input, jnp.zeros((1, feat_width), jnp.bfloat16)], axis=0)
    grad_pad = jnp.concatenate(
        [incoming_gradient.astype(jnp.float32), jnp.zeros((1, feat_width), jnp.float32)], axis=0
    )
    weight_pad = jnp.concatenate([weights.reshape(-1), jnp.zeros((1,), jnp.float32)])
    inputs_slab = normed_pad[token_of].reshape(experts, capacity, feat_width)
    grads_slab = (
        (weight_pad[source_of][:, None] * grad_pad[token_of])
        .astype(jnp.bfloat16)
        .reshape(experts, capacity, feat_width)
    )
    returned = send_back(
        slab_backward(
            lax.all_to_all(inputs_slab, "expert", split_axis=0, concat_axis=0, tiled=True),
            lax.all_to_all(grads_slab, "expert", split_axis=0, concat_axis=0, tiled=True),
            gate_up,
            down_proj,
        )
    )
    gathered = returned.reshape(experts * capacity, feat_width)[slot_index].astype(jnp.float32)
    dnorm = jnp.sum(gathered.reshape(tok_count, top_count, feat_width), axis=1)
    normalized_input_gradient = dnorm * gain_vector_row[None, :]
    projected_rows = jnp.mean(normalized_input_gradient * normalized_input, axis=-1, keepdims=True)
    section_gradient = (
        incoming_gradient.astype(jnp.float32)
        + inverse_root_mean * (normalized_input_gradient - normalized_input * projected_rows)
    ).astype(jnp.bfloat16)
    return shifted(section_gradient[None], "section", -1)


def solution(mesh):
    return jax.shard_map(
        per_device,
        mesh=mesh,
        in_specs=(
            P("section", "expert", None),
            P("section", None),
            P("section", "expert", None),
            P("section", "expert", None),
            P("section", "expert", None),
            P("section", "expert", None, None),
            P("section", "expert", None, None),
        ),
        out_specs=P("section", "expert", None),
        check_vma=False,
    )
```

profile of v0, /device:TPU:0, one launch (start us, length us, event | category | flops | bytes accessed | tf_op | source)
XLA Modules:
  0.0 365.0 jit_solution(3176427391684686881)
XLA Ops:
  0.0 0.8 copy.26
  0.8 0.1 eq.29
  0.9 0.1 eq.25
  1.0 0.7 broadcast_multiply_fusion
  1.7 1.1 reduce-window.6
  2.8 0.2 slice_reduce_fusion
  3.1 0.1 copy.25
  3.2 0.1 mul.118
  3.3 0.1 fusion.28
  3.4 2.4 scatter_custom_fusion
  5.9 1.5 copy.23
  7.4 0.2 fusion.21
  7.6 0.7 reduce.1
  8.4 0.2 fusion.19
  8.6 0.1 concatenate.18
  8.7 4.6 %gather_fusion.2 = bf16[640,2880]{1,0:T(8,128)(2,1)} fusion(bf16[129,2880]{1,0:T(8,128)(2,1)S(1)} %concatenate.18, s32[1024]{0:T(1024)S(1)} %get-tuple-element.9), kind=kCustom, calls=%fused_computation.2 | custom fusion | bytes 7375360 | tf_op jit(solution)/shard_map/gather | solution.py:84
  13.3 0.0 copy-start
  13.3 6.5 %all-to-all-start.1 = ((bf16[8,80,2880]{2,1,0:T(8,128)(2,1)}), bf16[8,80,2880]{2,1,0:T(8,128)(2,1)}, u32[]{:S(2)}, u32[]{:S(2)}) async-start(bf16[8,80,2880]{2,1,0:T(8,128)(2,1)} %bitcast.52), calls=%async_computation.1 | async-start | bytes 7536640 | tf_op jit(solution)/shard_map/all_to_all | solution.py:92
  19.8 0.0 copy-done
  19.8 0.3 copy.22
  20.1 0.1 pad_convert_fusion
  20.2 0.0 copy-start.1
  20.2 5.6 %gather_fusion.1 = f32[640,2880]{1,0:T(8,128)} fusion(f32[129,2880]{1,0:T(8,128)S(1)} %pad_convert_fusion, s32[1024]{0:T(1024)S(1)} %get-tuple-element.9), kind=kCustom, calls=%fused_computation.1 | custom fusion | bytes 14748160 | tf_op jit(solution)/shard_map/gather | solution.py:86
  25.9 0.0 copy-done.1
  25.9 0.1 copy.24
  26.0 0.1 reshape_squeeze.4
  26.1 2.8 gather_fusion
  28.9 0.1 mul.120
  29.0 5.9 %multiply_convert_fusion = bf16[8,80,2880]{2,1,0:T(8,128)(2,1)} fusion(f32[8,80,2880]{2,1,0:T(8,128)} %bitcast.51, f32[8,80]{1,0:T(8,128)S(1)} %mul.120), kind=kLoop, calls=%fused_computation.11 | loop fusion | flops 3686400 | bytes 11061760 | tf_op jit(solution)/shard_map/convert_element_type | solution.py:87
  34.8 69.9 %all-to-all-done.1 = bf16[8,80,2880]{2,1,0:T(8,128)(2,1)} async-done(((bf16[8,80,2880]{2,1,0:T(8,128)(2,1)}), bf16[8,80,2880]{2,1,0:T(8,128)(2,1)}, u32[]{:S(2)}, u32[]{:S(2)}) %all-to-all-start.1) | async-done | bytes 3686432 | tf_op jit(solution)/shard_map/all_to_all | solution.py:92
  104.7 4.7 %all-to-all-start = ((bf16[8,80,2880]{2,1,0:T(8,128)(2,1)}), bf16[8,80,2880]{2,1,0:T(8,128)(2,1)}, u32[]{:S(2)}, u32[]{:S(2)}) async-start(bf16[8,80,2880]{2,1,0:T(8,128)(2,1)} %multiply_convert_fusion), calls=%async_computation | async-start | bytes 7536640 | tf_op jit(solution)/shard_map/all_to_all | solution.py:93
  109.4 20.0 %fusion.2 = f32[640,2880]{0,1:T(8,128)} fusion(bf16[640,2880]{1,0:T(8,128)(2,1)} %bitcast.10, bf16[1,1,2880,2880]{3,2,1,0:T(8,128)(2,1)} %param.12), kind=kOutput, calls=%fused_computation.7 | convolution fusion | flops 10616832000 | bytes 27648000 | tf_op jit(solution)/shard_map/dot_general | solution.py:17
  129.4 64.7 %all-to-all-done = bf16[8,80,2880]{2,1,0:T(8,128)(2,1)} async-done(((bf16[8,80,2880]{2,1,0:T(8,128)(2,1)}), bf16[8,80,2880]{2,1,0:T(8,128)(2,1)}, u32[]{:S(2)}, u32[]{:S(2)}) %all-to-all-start) | async-done | bytes 3686432 | tf_op jit(solution)/shard_map/all_to_all | solution.py:93
  194.1 13.0 %fusion.11 = (bf16[640,1440]{0,1:T(8,128)(2,1)S(1)}, bf16[640,1440]{0,1:T(8,128)(2,1)S(1)}) fusion(f32[640,2880]{0,1:T(8,128)} %fusion.2, bf16[640,2880]{1,0:T(8,128)(2,1)} %bitcast.7, bf16[1,1,1440,2880]{3,2,1,0:T(8,128)(2,1)} %param.13), kind=kOutput, calls=%fused_computation.16 | convolution fusion | flops 5322240000 | bytes 23040000 | tf_op jit(solution)/shard_map/dot_general | solution.py:18
  207.2 17.8 %fusion.6 = bf16[640,2880]{0,1:T(8,128)(2,1)} fusion(bf16[1,1,2880,2880]{3,2,1,0:T(8,128)(2,1)} %param.12, bf16[640,1440]{0,1:T(8,128)(2,1)S(1)} %get-tuple-element.6, bf16[640,1440]{0,1:T(8,128)(2,1)S(1)} %get-tuple-element.5), kind=kOutput, calls=%fused_computation.12 | convolution fusion | flops 10626048000 | bytes 23961600 | tf_op jit(solution)/shard_map/dot_general | solution.py:28
  224.9 6.2 %copy.29 = bf16[640,2880]{1,0:T(8,128)(2,1)} copy(bf16[640,2880]{0,1:T(8,128)(2,1)} %fusion.6) | data formatting | bytes 7372800 | tf_op jit(solution)/shard_map/convert_element_type | solution.py:31
  231.1 4.7 %all-to-all-start.2 = ((bf16[8,80,2880]{2,1,0:T(8,128)(2,1)}), bf16[8,80,2880]{2,1,0:T(8,128)(2,1)}, u32[]{:S(2)}, u32[]{:S(2)}) async-start(bf16[8,80,2880]{2,1,0:T(8,128)(2,1)} %bitcast.53), calls=%async_computation.2 | async-start | bytes 7536640 | tf_op jit(solution)/shard_map/all_to_all | solution.py:46
  235.8 84.6 %all-to-all-done.2 = bf16[8,80,2880]{2,1,0:T(8,128)(2,1)} async-done(((bf16[8,80,2880]{2,1,0:T(8,128)(2,1)}), bf16[8,80,2880]{2,1,0:T(8,128)(2,1)}, u32[]{:S(2)}, u32[]{:S(2)}) %all-to-all-start.2) | async-done | bytes 3686432 | tf_op jit(solution)/shard_map/all_to_all | solution.py:46
  320.5 9.4 %gather_fusion.3 = bf16[512,2880]{1,0:T(8,128)(2,1)} fusion(bf16[640,2880]{1,0:T(8,128)(2,1)} %bitcast.13, s32[1024]{0:T(1024)S(1)} %pad_clamp_fusion), kind=kCustom, calls=%fused_computation.3 | custom fusion | bytes 5900288 | tf_op jit(solution)/shard_map/gather | solution.py:98
  329.9 6.5 %reshape.147 = f32[128,4,2880]{2,1,0:T(4,128)} reshape(bf16[512,2880]{1,0:T(8,128)(2,1)} %gather_fusion.3) | data formatting | bytes 8847360 | tf_op jit(solution)/shard_map/convert_element_type | solution.py:98
  336.4 6.3 %reduce_sum.43 = f32[128,2880]{1,0:T(8,128)S(1)} reduce(f32[128,4,2880]{2,1,0:T(4,128)} %reshape.147, f32[]{:T(128)} %constant.17.clone.1), dimensions={1}, to_apply=%region_5.6 | reduce | flops 1105920 | bytes 7372804 | tf_op jit(solution)/shard_map/reduce_sum | solution.py:99
  342.7 0.4 fusion.20
  343.1 1.4 fusion.26
  344.5 1.5 copy.30
  346.0 2.5 collective-permute-start
  348.5 15.6 %collective-permute-done = bf16[1,128,2880]{1,2,0:T(8,128)(2,1)S(1)} collective-permute-done((bf16[1,128,2880]{1,2,0:T(8,128)(2,1)S(1)}, bf16[1,128,2880]{1,2,0:T(8,128)(2,1)S(1)}, u32[]{:S(2)}, u32[]{:S(2)}) %collective-permute-start) | collective-permute-done | bytes 737312 | tf_op jit(solution)/shard_map/ppermute | solution.py:13
  364.1 0.9 copy.32
  (11 shorter events, 0.1 us)
Async XLA Ops:
  13.3 6.5 %copy-start = (bf16[1,128,2880]{1,2,0:T(8,128)(2,1)S(1)}, bf16[1,128,2880]{1,2,0:T(8,128)(2,1)}, u32[]{:S(2)}) copy-start(bf16[1,128,2880]{1,2,0:T(8,128)(2,1)} %param.9) | copy-start | bytes 2211844
  13.3 91.4 %all-to-all-start.1 = ((bf16[8,80,2880]{2,1,0:T(8,128)(2,1)}), bf16[8,80,2880]{2,1,0:T(8,128)(2,1)}, u32[]{:S(2)}, u32[]{:S(2)}) async-start(bf16[8,80,2880]{2,1,0:T(8,128)(2,1)} %bitcast.52), calls=%async_computation.1 | async-start | bytes 7536640 | tf_op jit(solution)/shard_map/all_to_all | solution.py:92
  20.2 5.6 %copy-start.1 = (f32[1,128,4]{1,2,0:T(4,128)S(1)}, f32[1,128,4]{1,2,0:T(4,128)}, u32[]{:S(2)}) copy-start(f32[1,128,4]{1,2,0:T(4,128)} %param.11) | copy-start | bytes 6148
  104.7 89.4 %all-to-all-start = ((bf16[8,80,2880]{2,1,0:T(8,128)(2,1)}), bf16[8,80,2880]{2,1,0:T(8,128)(2,1)}, u32[]{:S(2)}, u32[]{:S(2)}) async-start(bf16[8,80,2880]{2,1,0:T(8,128)(2,1)} %multiply_convert_fusion), calls=%async_computation | async-start | bytes 7536640 | tf_op jit(solution)/shard_map/all_to_all | solution.py:93
  231.1 89.4 %all-to-all-start.2 = ((bf16[8,80,2880]{2,1,0:T(8,128)(2,1)}), bf16[8,80,2880]{2,1,0:T(8,128)(2,1)}, u32[]{:S(2)}, u32[]{:S(2)}) async-start(bf16[8,80,2880]{2,1,0:T(8,128)(2,1)} %bitcast.53), calls=%async_computation.2 | async-start | bytes 7536640 | tf_op jit(solution)/shard_map/all_to_all | solution.py:46
  346.0 18.1 %collective-permute-start = (bf16[1,128,2880]{1,2,0:T(8,128)(2,1)S(1)}, bf16[1,128,2880]{1,2,0:T(8,128)(2,1)S(1)}, u32[]{:S(2)}, u32[]{:S(2)}) collective-permute-start(bf16[1,128,2880]{1,2,0:T(8,128)(2,1)S(1)} %copy.30), channel_id=1, source_target_pairs={{0,24},{8,0},{16,8},{24,16},{1,25},{9,1},{17,9},{25,17},{2,26},{10... | collective-permute-start | bytes 2211848 | tf_op jit(solution)/shard_map/ppermute | solution.py:13
where the time goes:
time: 366 us; the launch traced here: 365 us
  waiting for transfers between devices  235 us (64%)
  matrix products  50.8 us (14%)
  local copies, waits for them, and re-layouts  43.5 us (12%)
  starting transfers between devices  18.4 us (5%)
  other arithmetic  17.3 us (5%)
    all_to_all x1, waiting for transfers between devices, send_back(): lax.all_to_all(slab, 'expert', split_axis=0, concat_axis=0, tiled=True)  84.6 us
    all_to_all x1, waiting for transfers between devices, per_device(): lax.all_to_all(inputs_slab, 'expert', split_axis=0, concat_axis=0, tiled=...  69.9 us
    all_to_all x1, waiting for transfers between devices, per_device(): lax.all_to_all(grads_slab, 'expert', split_axis=0, concat_axis=0, tiled=T...  64.7 us
    dot_general x1, matrix products, expert_backward(): preact = jnp.dot(rows_in, gate_up, preferred_element_type=jnp.float32)  20 us
    dot_general x1, matrix products, expert_backward(): lax.dot_general(dpre, gate_up, (((1,), (1,)), ((), ())), preferred_elemen...  17.8 us
    ppermute x1, waiting for transfers between devices, shifted(): return lax.ppermute(value, axis, pairs)  15.6 us
    dot_general x1, matrix products, expert_backward(): lax.dot_general(grad_rows, down_proj, (((1,), (1,)), ((), ())), preferred...  13 us
    gather x1, local copies, waits for them, and re-layouts, per_device(): returned.reshape(experts * capacity, feat_width)[slot_index]  9.39 us
  transfers between devices with their start and end apart: 4, of which 4 were waited for; matrix products, arithmetic and copies ran while one was open for 10% of the time, Pallas kernels for 0%

commit v1 on v0

v1 whole, which is shorter than its diff:
```python
import functools
import jax
import jax.numpy as jnp
from jax import lax
from jax.experimental import pallas as pl
from jax.experimental.pallas import tpu as pltpu
from jax.sharding import PartitionSpec as P

glu_alpha = 1.702
norm_eps = 1e-05
vmem_bytes = 60 * 1024 * 1024


def spans(total, width):
    return [(start, min(start + width, total)) for start in range(0, total, width)]


def shifted(value, axis, steps):
    count = lax.axis_size(axis)
    pairs = [(source, (source + steps) % count) for source in range(count)]
    return lax.ppermute(value, axis, pairs)


def block_kernel(
    chips,
    x_hbm, g_hbm, wtab_hbm, gate_up_hbm, down_hbm, out_ref,
    xs, gs, wtab, ws, gate_up, down, pre, act, res, cross_in, line_in,
    load_sems, recv_x, recv_g, recv_w, send_w,
    up_x, up_g, dn_x, dn_g, cr_x, cr_g,
    cross_recv, cross_send, line_recv, line_send,
):
    me = lax.axis_index("expert")
    p = me // 2
    c = me % 2
    other = 1 - c
    count = 2 * chips
    rows, width = x_hbm.shape
    half = down_hbm.shape[0]
    out_spans = spans(width, 768)

    def device(chip, core):
        return {"expert": 2 * chip + core}

    load_x = pltpu.make_async_copy(x_hbm, xs.at[me], load_sems.at[0])
    load_g = pltpu.make_async_copy(g_hbm, gs.at[me], load_sems.at[1])
    load_w = pltpu.make_async_copy(wtab_hbm, wtab, load_sems.at[2])
    load_gate_up = pltpu.make_async_copy(gate_up_hbm, gate_up, load_sems.at[3])
    load_down = pltpu.make_async_copy(down_hbm, down, load_sems.at[4])
    load_x.start()
    load_g.start()
    load_w.start()
    load_gate_up.start()
    load_down.start()

    barrier = pltpu.get_barrier_semaphore()

    @pl.loop(1, count)
    def _(step):
        pl.semaphore_signal(barrier, inc=1, device_id={"expert": (me + step) % count})

    pl.semaphore_wait(barrier, count - 1)

    def gather_copy(buf, slot, send, recv, chip, core):
        return pltpu.make_async_remote_copy(
            src_ref=buf.at[slot], dst_ref=buf.at[slot],
            send_sem=send.at[slot], recv_sem=recv.at[slot],
            device_id=device(chip, core),
        )

    def weight_copy(target):
        return pltpu.make_async_remote_copy(
            src_ref=wtab.at[target], dst_ref=ws.at[me],
            send_sem=send_w.at[target], recv_sem=recv_w.at[me],
            device_id={"expert": target},
        )

    def weight_arrival(source):
        return pltpu.make_async_remote_copy(
            src_ref=wtab.at[source], dst_ref=ws.at[source],
            send_sem=send_w.at[source], recv_sem=recv_w.at[source],
            device_id={"expert": source},
        )

    def up_copy(buf, slot, send, recv):
        return gather_copy(buf, slot, send, recv, jnp.minimum(p + 1, chips - 1), c)

    def down_copy(buf, slot, send, recv):
        return gather_copy(buf, slot, send, recv, jnp.maximum(p - 1, 0), c)

    def core_copy(buf, slot, send, recv):
        return gather_copy(buf, slot, send, recv, p, other)

    def send_own(buf, up_sem, dn_sem, recv):
        @pl.when(p < chips - 1)
        def _():
            up_copy(buf, me, up_sem, recv).start()

        @pl.when(p > 0)
        def _():
            down_copy(buf, me, dn_sem, recv).start()

    def pass_on(k, buf, up_sem, dn_sem, cr_sem, recv):
        @pl.when(p - k >= 0)
        def _():
            slot = 2 * (p - k) + c
            core_copy(buf, slot, cr_sem, recv).wait_recv()
            core_copy(buf, slot, cr_sem, recv).start()

            @pl.when(p < chips - 1)
            def _():
                up_copy(buf, slot, up_sem, recv).start()

        @pl.when(p + k < chips)
        def _():
            slot = 2 * (p + k) + c
            core_copy(buf, slot, cr_sem, recv).wait_recv()
            core_copy(buf, slot, cr_sem, recv).start()

            @pl.when(p > 0)
            def _():
                down_copy(buf, slot, dn_sem, recv).start()

    def cross_copy(q, t):
        first, last = out_spans[t]
        return pltpu.make_async_remote_copy(
            src_ref=res.at[2 * q + other, :, pl.ds(first, last - first)],
            dst_ref=cross_in.at[q, :, pl.ds(first, last - first)],
            send_sem=cross_send.at[q, t], recv_sem=cross_recv.at[q, t],
            device_id=device(p, other),
        )

    def cross_arrival(q, t):
        return cross_copy(q, t)

    def line_copy(q, t):
        first, last = out_spans[t]
        toward = jnp.where(q > p, jnp.minimum(p + 1, chips - 1), jnp.maximum(p - 1, 0))
        slot = jnp.where(q > p, 0, 1)
        return pltpu.make_async_remote_copy(
            src_ref=res.at[2 * q + c, :, pl.ds(first, last - first)],
            dst_ref=line_in.at[slot, q, :, pl.ds(first, last - first)],
            send_sem=line_send.at[q, t], recv_sem=line_recv.at[slot, q, t],
            device_id=device(toward, c),
        )

    def line_arrival(slot, q, t):
        first, last = out_spans[t]
        return pltpu.make_async_remote_copy(
            src_ref=res.at[2 * q + c, :, pl.ds(first, last - first)],
            dst_ref=line_in.at[slot, q, :, pl.ds(first, last - first)],
            send_sem=line_send.at[q, t], recv_sem=line_recv.at[slot, q, t],
            device_id=device(p, other),
        )

    def combine(q, t):
        first, last = out_spans[t]
        cross_arrival(q, t).wait_recv()
        summed = res[2 * q + c, :, first:last].astype(jnp.float32) + cross_in[
            q, :, first:last
        ].astype(jnp.float32)
        res[2 * q + c, :, first:last] = summed.astype(jnp.bfloat16)
        starts = ((p == chips - 1) & (q < p)) | ((p == 0) & (q > p))

        @pl.when(starts)
        def _():
            line_copy(q, t).start()

    load_x.wait()
    core_copy(xs, me, cr_x, recv_x).start()
    send_own(xs, up_x, dn_x, recv_x)
    load_g.wait()
    core_copy(gs, me, cr_g, recv_g).start()
    load_w.wait()

    @pl.loop(1, count)
    def _(step):
        weight_copy((me + step) % count).start()

    ws[pl.ds(me, 1)] = wtab[pl.ds(me, 1)]
    load_gate_up.wait()
    load_down.wait()

    @pl.loop(1, count)
    def _(step):
        weight_arrival((me + step) % count).wait_recv()

    def forward_part(q):
        core_copy(xs, 2 * q + other, cr_x, recv_x).wait_recv()
        inputs = xs[pl.ds(2 * q, 2)].reshape(2 * rows, width)
        for first, last in spans(2 * half, 512):
            pre[:, first:last] = jnp.dot(
                inputs, gate_up[:, first:last], preferred_element_type=jnp.float32
            )

    def backward_part(q):
        core_copy(gs, 2 * q + other, cr_g, recv_g).wait_recv()
        diagonal = lax.broadcasted_iota(jnp.int32, (rows, rows), 0) == lax.broadcasted_iota(
            jnp.int32, (rows, rows), 1
        )
        for core in range(2):
            across = jnp.broadcast_to(ws[2 * q + core], (rows, rows))
            column = jnp.sum(jnp.where(diagonal, across, 0.0), axis=1, keepdims=True)
            act[core * rows:(core + 1) * rows, :] = (
                column * gs[2 * q + core].astype(jnp.float32)
            ).astype(jnp.bfloat16)
        for first, last in spans(half, 512):
            dact = lax.dot_general(
                act[...], down[first:last, :], (((1,), (1,)), ((), ())),
                preferred_element_type=jnp.float32,
            )
            gate = pre[:, first:last]
            up_part = pre[:, half + first:half + last]
            sig = jax.nn.sigmoid(glu_alpha * gate)
            pre[:, first:last] = dact * (up_part + 1.0) * (
                sig + glu_alpha * gate * sig * (1.0 - sig)
            )
            pre[:, half + first:half + last] = dact * gate * sig
        act[...] = pre[...].astype(jnp.bfloat16)
        for t, (first, last) in enumerate(out_spans):
            part = lax.dot_general(
                act[...], gate_up[first:last, :], (((1,), (1,)), ((), ())),
                preferred_element_type=jnp.float32,
            ).astype(jnp.bfloat16)
            res[pl.ds(2 * q, 2), :, first:last] = part.reshape(2, rows, last - first)
            cross_copy(q, t).start()
            if t > 0:
                combine(q, t - 1)
        combine(q, len(out_spans) - 1)

    @pl.loop(0, 2 * chips - 1)
    def _(i):
        k = (i + 1) // 2
        leading = i % 2 == 1
        q = jnp.where(leading, p - k, p + k)
        valid = (q >= 0) & (q < chips)

        @pl.when(leading)
        def _():
            pass_on(k, xs, up_x, dn_x, cr_x, recv_x)

        @pl.when(valid)
        def _():
            forward_part(q)

        @pl.when(leading)
        def _():
            pass_on(k, gs, up_g, dn_g, cr_g, recv_g)

        @pl.when(i == 0)
        def _():
            send_own(gs, up_g, dn_g, recv_g)

        @pl.when(valid)
        def _():
            backward_part(q)

    def relay(slot, q, t):
        first, last = out_spans[t]
        line_arrival(slot, q, t).wait_recv()
        summed = res[2 * q + c, :, first:last].astype(jnp.float32) + line_in[
            slot, q, :, first:last
        ].astype(jnp.float32)
        res[2 * q + c, :, first:last] = summed.astype(jnp.bfloat16)
        line_copy(q, t).start()

    inner = (p > 0) & (p < chips - 1)
    near_low = p < chips // 2
    for distance in range(1, chips):
        for t in range(len(out_spans)):
            for turn in range(2):
                slot = jnp.where(near_low, turn, 1 - turn)
                q = jnp.where(slot == 0, distance, chips - 1 - distance)
                ahead = jnp.where(slot == 0, q > p, q < p)

                @pl.when(inner & ahead)
                def _(slot=slot, q=q, t=t):
                    relay(slot, q, t)

    for t, (first, last) in enumerate(out_spans):
        out_ref[:, first:last] = res[me, :, first:last].astype(jnp.float32)

        @pl.when(p > 0)
        def _(t=t, first=first, last=last):
            line_arrival(0, p, t).wait_recv()
            out_ref[:, first:last] += line_in[0, p, :, first:last].astype(jnp.float32)

        @pl.when(p < chips - 1)
        def _(t=t, first=first, last=last):
            line_arrival(1, p, t).wait_recv()
            out_ref[:, first:last] += line_in[1, p, :, first:last].astype(jnp.float32)

    @pl.loop(1, count)
    def _(step):
        weight_copy((me + step) % count).wait_send()

    @pl.loop(0, chips)
    def _(q):
        slot = 2 * q + c
        core_copy(xs, slot, cr_x, recv_x).wait_send()
        core_copy(gs, slot, cr_g, recv_g).wait_send()

        @pl.when((q <= p) & (p < chips - 1))
        def _():
            up_copy(xs, slot, up_x, recv_x).wait_send()
            up_copy(gs, slot, up_g, recv_g).wait_send()

        @pl.when((q >= p) & (p > 0))
        def _():
            down_copy(xs, slot, dn_x, recv_x).wait_send()
            down_copy(gs, slot, dn_g, recv_g).wait_send()

        for t in range(len(out_spans)):
            cross_copy(q, t).wait_send()

            @pl.when(q != p)
            def _(t=t):
                line_copy(q, t).wait_send()


def line_backward(normed, grads, weight_table, gate_up, down_proj):
    count = weight_table.shape[0]
    chips = count // 2
    rows, width = normed.shape
    half = down_proj.shape[0]
    pieces = len(spans(width, 768))
    dma = pltpu.SemaphoreType.DMA
    flops = 2 * count * rows * width * 5 * half
    return pl.pallas_call(
        functools.partial(block_kernel, chips),
        out_shape=jax.ShapeDtypeStruct((rows, width), jnp.float32),
        in_specs=[pl.BlockSpec(memory_space=pl.ANY)] * 5,
        out_specs=pl.BlockSpec(memory_space=pltpu.VMEM),
        scratch_shapes=[
            pltpu.VMEM((count, rows, width), jnp.bfloat16),
            pltpu.VMEM((count, rows, width), jnp.bfloat16),
            pltpu.VMEM((count, 1, rows), jnp.float32),
            pltpu.VMEM((count, 1, rows), jnp.float32),
            pltpu.VMEM((width, 2 * half), jnp.bfloat16),
            pltpu.VMEM((half, width), jnp.bfloat16),
            pltpu.VMEM((2 * rows, 2 * half), jnp.float32),
            pltpu.VMEM((2 * rows, width), jnp.bfloat16),
            pltpu.VMEM((count, rows, width), jnp.bfloat16),
            pltpu.VMEM((chips, rows, width), jnp.bfloat16),
            pltpu.VMEM((2, chips, rows, width), jnp.bfloat16),
            dma((5,)),
            dma((count,)), dma((count,)), dma((count,)), dma((count,)),
            dma((count,)), dma((count,)), dma((count,)), dma((count,)),
            dma((count,)), dma((count,)),
            dma((chips, pieces)), dma((chips, pieces)),
            dma((2, chips, pieces)), dma((chips, pieces)),
        ],
        compiler_params=pltpu.CompilerParams(
            collective_id=0, has_side_effects=True, vmem_limit_bytes=vmem_bytes
        ),
        cost_estimate=pl.CostEstimate(
            flops=flops, bytes_accessed=10 * half * width, transcendentals=0
        ),
    )(normed, grads, weight_table, gate_up, down_proj)


def expert_backward(rows_in, grad_rows, gate_up, down_proj):
    preact = jnp.dot(rows_in, gate_up, preferred_element_type=jnp.float32)
    dact = lax.dot_general(
        grad_rows, down_proj, (((1,), (1,)), ((), ())), preferred_element_type=jnp.float32
    )
    half = down_proj.shape[0]
    gate = preact[:, :half]
    up_part = preact[:, half:]
    sig = jax.nn.sigmoid(glu_alpha * gate)
    dgate = dact * (up_part + 1.0) * (sig + glu_alpha * gate * sig * (1.0 - sig))
    dup = dact * gate * sig
    dpre = jnp.concatenate([dgate, dup], axis=1).astype(jnp.bfloat16)
    result = lax.dot_general(
        dpre, gate_up, (((1,), (1,)), ((), ())), preferred_element_type=jnp.float32
    )
    return result.astype(jnp.bfloat16)


def slab_exchange(slab):
    return lax.all_to_all(slab, "expert", split_axis=0, concat_axis=0, tiled=True)


def slab_backward(normed, grads, routes, weights, gate_up, down_proj, experts):
    tok_count, feat_width = normed.shape
    top_count = routes.shape[1]
    capacity = max(2, tok_count * top_count * 5 // (4 * experts))
    flat_ids = routes.reshape(-1)
    assign = flat_ids.shape[0]
    one_hot = (flat_ids[:, None] == jnp.arange(experts, dtype=jnp.int32)[None, :]).astype(jnp.int32)
    slot_rank = jnp.sum((jnp.cumsum(one_hot, axis=0) - one_hot) * one_hot, axis=1)
    slot_index = flat_ids * capacity + slot_rank
    source_of = (
        jnp.full((experts * capacity,), assign, jnp.int32)
        .at[slot_index]
        .set(jnp.arange(assign, dtype=jnp.int32))
    )
    token_of = source_of // top_count
    normed_pad = jnp.concatenate([normed, jnp.zeros((1, feat_width), jnp.bfloat16)], axis=0)
    grad_pad = jnp.concatenate(
        [grads.astype(jnp.float32), jnp.zeros((1, feat_width), jnp.float32)], axis=0
    )
    weight_pad = jnp.concatenate([weights.reshape(-1), jnp.zeros((1,), jnp.float32)])
    inputs_slab = normed_pad[token_of].reshape(experts, capacity, feat_width)
    grads_slab = (
        (weight_pad[source_of][:, None] * grad_pad[token_of])
        .astype(jnp.bfloat16)
        .reshape(experts, capacity, feat_width)
    )
    worked = expert_backward(
        slab_exchange(inputs_slab).reshape(experts * capacity, feat_width),
        slab_exchange(grads_slab).reshape(experts * capacity, feat_width),
        gate_up,
        down_proj,
    )
    returned = slab_exchange(worked.reshape(experts, capacity, feat_width))
    gathered = returned.reshape(experts * capacity, feat_width)[slot_index].astype(jnp.float32)
    return jnp.sum(gathered.reshape(tok_count, top_count, feat_width), axis=1)


def per_device(hidden_in, norm_gain, out_grad, expert_ids, route_weights, w_gate_up, w_down):
    tokens = hidden_in[0]
    gain_vector_row = norm_gain[0]
    incoming_gradient = out_grad[0]
    routes = expert_ids[0]
    weights = route_weights[0]
    gate_up = w_gate_up[0, 0]
    down_proj = w_down[0, 0]
    experts = lax.axis_size("expert")
    input_single_precision = tokens.astype(jnp.float32)
    inverse_root_mean = lax.rsqrt(
        jnp.mean(input_single_precision * input_single_precision, axis=-1, keepdims=True) + norm_eps
    )
    normalized_input = input_single_precision * inverse_root_mean
    rescaled_input = (normalized_input * gain_vector_row[None, :]).astype(jnp.bfloat16)
    block = tokens.size * 2
    held = gate_up.size * 2 + down_proj.size * 2 + (4 * experts + 9) * block
    if experts % 2 == 0 and held < vmem_bytes:
        chosen = routes[None, :, :] == jnp.arange(experts, dtype=jnp.int32)[:, None, None]
        weight_table = jnp.sum(jnp.where(chosen, weights[None, :, :], 0.0), axis=-1)
        dnorm = line_backward(
            rescaled_input, incoming_gradient, weight_table[:, None, :], gate_up, down_proj
        )
    else:
        dnorm = slab_backward(
            rescaled_input, incoming_gradient, routes, weights, gate_up, down_proj, experts
        )
    normalized_input_gradient = dnorm * gain_vector_row[None, :]
    projected_rows = jnp.mean(normalized_input_gradient * normalized_input, axis=-1, keepdims=True)
    section_gradient = (
        incoming_gradient.astype(jnp.float32)
        + inverse_root_mean * (normalized_input_gradient - normalized_input * projected_rows)
    ).astype(jnp.bfloat16)
    return shifted(section_gradient[None], "section", -1)


def solution(mesh):
    return jax.shard_map(
        per_device,
        mesh=mesh,
        in_specs=(
            P("section", "expert", None),
            P("section", None),
            P("section", "expert", None),
            P("section", "expert", None),
            P("section", "expert", None),
            P("section", "expert", None, None),
            P("section", "expert", None, None),
        ),
        out_specs=P("section", "expert", None),
        check_vma=False,
    )
```

time: 366 us -> 180 us (0.49)
  waiting for transfers between devices: 235 us -> 11.9 us
  Pallas kernels: 0 us -> 157 us
  matrix products: 50.8 us -> 0 us
  local copies, waits for them, and re-layouts: 43.5 us -> 4 us
  starting transfers between devices: 18.4 us -> 2.49 us
  other arithmetic: 17.3 us -> 4.47 us
    all_to_all x3 -> x0, waiting for transfers between devices: 219 us -> none  [the longest x1 84.6 us: send_back(): lax.all_to_all(slab, 'expert', split_axis=0, concat_axis=0, tiled=True)]
    pallas_call x0 -> x1, Pallas kernels: none -> 157 us  [line_backward(): pl.pallas_call(functools.partial(block_kernel, chips), out_shape=jax.Shap...]
    dot_general x3 -> x0, matrix products: 50.8 us -> none  [the longest x1 20 us: expert_backward(): preact = jnp.dot(rows_in, gate_up, preferred_element_type=jnp.float32)]
    gather x4 -> x0, local copies, waits for them, and re-layouts: 22.4 us -> none  [the longest x1 9.39 us: per_device(): returned.reshape(experts * capacity, feat_width)[slot_index]]
    all_to_all x3 -> x0, starting transfers between devices: 15.9 us -> none  [the longest x1 6.46 us: per_device(): lax.all_to_all(inputs_slab, 'expert', split_axis=0, concat_axis=0, tiled=...]
    convert_element_type x3 -> x0, local copies, waits for them, and re-layouts: 14.2 us -> none  [the longest x1 6.54 us: per_device(): returned.reshape(experts * capacity, feat_width)[slot_index]]
    convert_element_type x3 -> x0, other arithmetic: 7.28 us -> none  [the longest x1 5.86 us: per_device(): grads_slab = (weight_pad[source_of][:, None] * grad_pad[token_of]).astype...]
    reduce_sum x2 -> x1, other arithmetic: 6.39 us -> 0.6 us  [per_device(): weight_table = jnp.sum(jnp.where(chosen, weights[None, :, :], 0.0), axis=-1)]
  transfers between devices with their start and end apart: 4 -> 1, of which waited for: 4 -> 1; matrix products, arithmetic and copies ran while one was open for 10% -> 0% of each run, Pallas kernels for 0% -> 0%
where the time goes in v1:
time: 180 us
  Pallas kernels  157 us (87%)
  waiting for transfers between devices  11.9 us (7%)
  other arithmetic  4.47 us (2%)
  local copies, waits for them, and re-layouts  4 us (2%)
  starting transfers between devices  2.49 us (1%)
    pallas_call x1, Pallas kernels, line_backward(): pl.pallas_call(functools.partial(block_kernel, chips), out_shape=jax.Shap...  157 us
    ppermute x1, waiting for transfers between devices, shifted(): return lax.ppermute(value, axis, pairs)  11.9 us
    unnamed x15, local copies, waits for them, and re-layouts  3.64 us
  transfers between devices with their start and end apart: 1, of which 1 were waited for; matrix products, arithmetic and copies ran while one was open for 0% of the time, Pallas kernels for 0%

profile of v1, /device:TPU:0, one launch (start us, length us, event | category | flops | bytes accessed | tf_op | source)
XLA Modules:
  0.0 180.2 jit_solution(8509577427162982411)
XLA Ops:
  0.0 0.0 copy-start.2
  0.0 0.0 copy-start.4
  0.0 0.0 copy-start.5
  0.0 0.0 copy-start.3
  0.0 1.5 copy.19
  1.5 0.2 fusion.9
  1.8 0.0 copy-done.2
  1.8 1.2 copy.18
  2.9 0.0 copy-done.4
  3.0 0.0 copy-done.5
  3.0 0.6 select_reduce_fusion
  3.6 0.0 copy-done.3
  3.6 1.1 fusion.3.x_hbm
  4.7 157.4 %shard_map.73 = f32[128,2880]{1,0:T(8,128)} custom-call(bf16[128,2880]{1,0:T(8,128)(2,1)} %fusion.3.x_hbm, bf16[128,2880]{1,0:T(8,128)(2,1)} %bitcast.15, f32[8,1,128]{2,1,0:T(1,128)} %bitcast.16, bf16[2880,2880]{1,0:T(8,128)(2,1)} %bitcast.19, bf16[1440,2880]{1,0:T(8,128)(2,1)} %bitcast.20), custom_call_target="tpu_custom_call" | custom-call | flops 42467328000 | bytes 41472000 | tf_op jit(solution)/shard_map/pallas_call | solution.py:328
  162.1 0.0 copy-start
  162.1 0.0 copy-start.1
  162.1 1.9 %fusion.4 = f32[128]{0:T(128)S(1)} fusion(f32[128,2880]{1,0:T(8,128)} %shard_map.73, bf16[1,128,2880]{2,1,0:T(8,128)(2,1)S(1)} %copy.19, f32[2880]{0:T(1024)S(1)} %reduce, f32[128]{0:T(128)S(1)} %add_rsqrt_fusion), kind=kLoop, calls=%fused_computation.6 | loop fusion | flops 1843072 | bytes 2224384 | tf_op jit(solution)/shard_map/reduce_sum | solution.py:448
  164.0 0.0 copy-done
  164.0 0.1 copy-done.1
  164.1 0.6 fusion.10
  164.7 0.4 copy.20
  165.0 2.5 %collective-permute-start = (bf16[1,128,2880]{1,2,0:T(8,128)(2,1)S(1)}, bf16[1,128,2880]{1,2,0:T(8,128)(2,1)S(1)}, u32[]{:S(2)}, u32[]{:S(2)}) collective-permute-start(bf16[1,128,2880]{1,2,0:T(8,128)(2,1)S(1)} %copy.20), channel_id=1, source_target_pairs={{0,24},{8,0},{16,8},{24,16},{1,25},{9,1},{17,9},{25,17},{2,26},{10... | collective-permute-start | bytes 2211848 | tf_op jit(solution)/shard_map/ppermute | solution.py:21
  167.5 11.9 %collective-permute-done = bf16[1,128,2880]{1,2,0:T(8,128)(2,1)S(1)} collective-permute-done((bf16[1,128,2880]{1,2,0:T(8,128)(2,1)S(1)}, bf16[1,128,2880]{1,2,0:T(8,128)(2,1)S(1)}, u32[]{:S(2)}, u32[]{:S(2)}) %collective-permute-start) | collective-permute-done | bytes 737312 | tf_op jit(solution)/shard_map/ppermute | solution.py:21
  179.4 0.9 copy.22
  (3 shorter events, 0.0 us)
Async XLA Ops:
  0.0 1.8 copy-start.2
  0.0 2.9 %copy-start.4 = (f32[1,128,4]{1,2,0:T(4,128)S(1)}, f32[1,128,4]{1,2,0:T(4,128)}, u32[]{:S(2)}) copy-start(f32[1,128,4]{1,2,0:T(4,128)} %param.11) | copy-start | bytes 6148
  0.0 2.9 %copy-start.5 = (s32[1,128,4]{1,2,0:T(4,128)S(1)}, s32[1,128,4]{1,2,0:T(4,128)}, u32[]{:S(2)}) copy-start(s32[1,128,4]{1,2,0:T(4,128)} %param.10) | copy-start | bytes 6148
  0.0 3.5 %copy-start.3 = (f32[1,2880]{1,0:T(1,128)S(1)}, f32[1,2880]{1,0:T(1,128)}, u32[]{:S(2)}) copy-start(f32[1,2880]{1,0:T(1,128)} %param.8) | copy-start | bytes 34564
  162.1 1.9 %copy-start = (f32[128,2880]{1,0:T(8,128)S(1)}, f32[128,2880]{1,0:T(8,128)}, u32[]{:S(2)}) copy-start(f32[128,2880]{1,0:T(8,128)} %shard_map.73) | copy-start | bytes 4423684
  162.1 2.0 %copy-start.1 = (bf16[1,128,2880]{2,1,0:T(8,128)(2,1)S(1)}, bf16[1,128,2880]{2,1,0:T(8,128)(2,1)}, u32[]{:S(2)}) copy-start(bf16[1,128,2880]{2,1,0:T(8,128)(2,1)} %copy.18) | copy-start | bytes 2211844
  165.0 14.3 %collective-permute-start = (bf16[1,128,2880]{1,2,0:T(8,128)(2,1)S(1)}, bf16[1,128,2880]{1,2,0:T(8,128)(2,1)S(1)}, u32[]{:S(2)}, u32[]{:S(2)}) collective-permute-start(bf16[1,128,2880]{1,2,0:T(8,128)(2,1)S(1)} %copy.20), channel_id=1, source_target_pairs={{0,24},{8,0},{16,8},{24,16},{1,25},{9,1},{17,9},{25,17},{2,26},{10... | collective-permute-start | bytes 2211848 | tf_op jit(solution)/shard_map/ppermute | solution.py:21

commit v2 on v1

--- a/solution.py
+++ b/solution.py
@@ -8,7 +8,8 @@
 
 glu_alpha = 1.702
 norm_eps = 1e-05
-vmem_bytes = 60 * 1024 * 1024
+vmem_bytes = 62 * 1024 * 1024
+tile_width = 512
 
 
 def spans(total, width):
@@ -23,30 +24,37 @@
 
 def block_kernel(
     chips,
-    x_hbm, g_hbm, wtab_hbm, gate_up_hbm, down_hbm, out_ref,
-    xs, gs, wtab, ws, gate_up, down, pre, act, res, cross_in, line_in,
-    load_sems, recv_x, recv_g, recv_w, send_w,
+    hidden_hbm, gain_hbm, grad_hbm, wtab_hbm, gate_up_hbm, down_hbm, out_ref,
+    xs, gs, gain, wtab, ws, gate_up, down, pre, act, res, cross_in, line_in,
+    next_hidden, next_grad, next_gain, next_sum, inverse,
+    load_sems, ahead_send, ahead_recv, sum_send, sum_recv, recv_x, recv_g, recv_w, send_w,
     up_x, up_g, dn_x, dn_g, cr_x, cr_g,
     cross_recv, cross_send, line_recv, line_send,
 ):
     me = lax.axis_index("expert")
+    section = lax.axis_index("section")
+    sections = lax.axis_size("section")
+    preceding = (section + sections - 1) % sections
+    following = (section + 1) % sections
     p = me // 2
     c = me % 2
     other = 1 - c
     count = 2 * chips
-    rows, width = x_hbm.shape
+    rows, width = hidden_hbm.shape[1:]
     half = down_hbm.shape[0]
-    out_spans = spans(width, 768)
+    out_spans = spans(width, tile_width)
 
     def device(chip, core):
         return {"expert": 2 * chip + core}
 
-    load_x = pltpu.make_async_copy(x_hbm, xs.at[me], load_sems.at[0])
-    load_g = pltpu.make_async_copy(g_hbm, gs.at[me], load_sems.at[1])
+    load_x = pltpu.make_async_copy(hidden_hbm.at[0], xs.at[me], load_sems.at[0])
+    load_g = pltpu.make_async_copy(grad_hbm.at[0], gs.at[me], load_sems.at[1])
     load_w = pltpu.make_async_copy(wtab_hbm, wtab, load_sems.at[2])
     load_gate_up = pltpu.make_async_copy(gate_up_hbm, gate_up, load_sems.at[3])
     load_down = pltpu.make_async_copy(down_hbm, down, load_sems.at[4])
+    load_gain = pltpu.make_async_copy(gain_hbm, gain, load_sems.at[5])
     load_x.start()
+    load_gain.start()
     load_g.start()
     load_w.start()
     load_gate_up.start()
@@ -58,7 +66,42 @@
     def _(step):
         pl.semaphore_signal(barrier, inc=1, device_id={"expert": (me + step) % count})
 
-    pl.semaphore_wait(barrier, count - 1)
+    for neighbour in (preceding, following):
+        pl.semaphore_signal(barrier, inc=1, device_id={"section": neighbour})
+
+    load_x.wait()
+    load_gain.wait()
+
+    @pl.loop(0, rows // 16)
+    def _(r):
+        part = pl.ds(r * 16, 16)
+        wide = xs[me, part, :].astype(jnp.float32)
+        scale = lax.rsqrt(jnp.mean(wide * wide, axis=-1, keepdims=True) + norm_eps)
+        xs[me, part, :] = (wide * scale * gain[...]).astype(jnp.bfloat16)
+
+    pl.semaphore_wait(barrier, count + 1)
+
+    def ahead_copy(number, source, target):
+        return pltpu.make_async_remote_copy(
+            src_ref=source, dst_ref=target,
+            send_sem=ahead_send.at[number], recv_sem=ahead_recv.at[number],
+            device_id={"section": preceding},
+        )
+
+    ahead = [
+        ahead_copy(0, hidden_hbm.at[0], next_hidden),
+        ahead_copy(1, grad_hbm.at[0], next_grad),
+        ahead_copy(2, gain_hbm, next_gain),
+    ]
+
+    def sum_copy(t):
+        first, last = out_spans[t]
+        return pltpu.make_async_remote_copy(
+            src_ref=res.at[me, :, pl.ds(first, last - first)],
+            dst_ref=next_sum.at[:, pl.ds(first, last - first)],
+            send_sem=sum_send.at[t], recv_sem=sum_recv.at[t],
+            device_id={"section": preceding},
+        )
 
     def gather_copy(buf, slot, send, recv, chip, core):
         return pltpu.make_async_remote_copy(
@@ -165,11 +208,12 @@
         def _():
             line_copy(q, t).start()
 
-    load_x.wait()
     core_copy(xs, me, cr_x, recv_x).start()
     send_own(xs, up_x, dn_x, recv_x)
     load_g.wait()
     core_copy(gs, me, cr_g, recv_g).start()
+    for copy in ahead:
+        copy.start()
     load_w.wait()
 
     @pl.loop(1, count)
@@ -227,24 +271,29 @@
                 combine(q, t - 1)
         combine(q, len(out_spans) - 1)
 
+    low = p < chips // 2
+
+    def chunk_of(k, first_turn):
+        return jnp.where(low == first_turn, p + k, p - k)
+
+    def inside(q):
+        return (q >= 0) & (q < chips)
+
     @pl.loop(0, 2 * chips - 1)
     def _(i):
         k = (i + 1) // 2
         leading = i % 2 == 1
-        q = jnp.where(leading, p - k, p + k)
-        valid = (q >= 0) & (q < chips)
-
-        @pl.when(leading)
-        def _():
-            pass_on(k, xs, up_x, dn_x, cr_x, recv_x)
+        q = chunk_of(k, leading)
+        valid = inside(q)
+        paired = inside(chunk_of(k - 1, False)) & (k >= 2)
 
         @pl.when(valid)
         def _():
             forward_part(q)
 
-        @pl.when(leading)
-        def _():
-            pass_on(k, gs, up_g, dn_g, cr_g, recv_g)
+        @pl.when((leading & jnp.logical_not(paired)) | (jnp.logical_not(leading) & valid & (i > 0)))
+        def _():
+            pass_on(jnp.where(leading, k, k + 1), gs, up_g, dn_g, cr_g, recv_g)
 
         @pl.when(i == 0)
         def _():
@@ -253,6 +302,10 @@
         @pl.when(valid)
         def _():
             backward_part(q)
+
+        @pl.when(leading | (i == 0))
+        def _():
+            pass_on(k + 1, xs, up_x, dn_x, cr_x, recv_x)
 
     def relay(slot, q, t):
         first, last = out_spans[t]
@@ -264,30 +317,64 @@
         line_copy(q, t).start()
 
     inner = (p > 0) & (p < chips - 1)
-    near_low = p < chips // 2
-    for distance in range(1, chips):
+
+    def relay_all(distance):
         for t in range(len(out_spans)):
             for turn in range(2):
-                slot = jnp.where(near_low, turn, 1 - turn)
+                slot = jnp.where(low, turn, 1 - turn)
                 q = jnp.where(slot == 0, distance, chips - 1 - distance)
-                ahead = jnp.where(slot == 0, q > p, q < p)
-
-                @pl.when(inner & ahead)
+                onward = jnp.where(slot == 0, q > p, q < p)
+
+                @pl.when(inner & onward)
                 def _(slot=slot, q=q, t=t):
                     relay(slot, q, t)
 
+    for distance in range(1, chips - 1):
+        relay_all(distance)
+
+    for copy in ahead:
+        copy.wait_recv()
+
+    @pl.loop(0, rows // 16)
+    def _(r):
+        part = pl.ds(r * 16, 16)
+        wide = next_hidden[part, :].astype(jnp.float32)
+        inverse[part, :] = lax.rsqrt(jnp.mean(wide * wide, axis=-1, keepdims=True) + norm_eps)
+
     for t, (first, last) in enumerate(out_spans):
-        out_ref[:, first:last] = res[me, :, first:last].astype(jnp.float32)
-
-        @pl.when(p > 0)
-        def _(t=t, first=first, last=last):
-            line_arrival(0, p, t).wait_recv()
-            out_ref[:, first:last] += line_in[0, p, :, first:last].astype(jnp.float32)
-
-        @pl.when(p < chips - 1)
-        def _(t=t, first=first, last=last):
-            line_arrival(1, p, t).wait_recv()
-            out_ref[:, first:last] += line_in[1, p, :, first:last].astype(jnp.float32)
+        for slot in range(2):
+            @pl.when((p > 0) if slot == 0 else (p < chips - 1))
+            def _(slot=slot, t=t, first=first, last=last):
+                line_arrival(slot, p, t).wait_recv()
+
+        below = jnp.where(p > 0, line_in[0, p, :, first:last].astype(jnp.float32), 0.0)
+        above = jnp.where(p < chips - 1, line_in[1, p, :, first:last].astype(jnp.float32), 0.0)
+        res[me, :, first:last] = (
+            res[me, :, first:last].astype(jnp.float32) + below + above
+        ).astype(jnp.bfloat16)
+        sum_copy(t).start()
+
+    relay_all(chips - 1)
+
+    scale = inverse[...]
+    projected = jnp.zeros((rows, 1), jnp.float32)
+    for t, (first, last) in enumerate(out_spans):
+        sum_copy(t).wait_recv()
+        slope = next_sum[:, first:last].astype(jnp.float32) * next_gain[:, first:last]
+        unit = next_hidden[:, first:last].astype(jnp.float32) * scale
+        projected += jnp.sum(slope * unit, axis=1, keepdims=True)
+    projected = projected / width
+    for first, last in out_spans:
+        slope = next_sum[:, first:last].astype(jnp.float32) * next_gain[:, first:last]
+        unit = next_hidden[:, first:last].astype(jnp.float32) * scale
+        out_ref[0, :, first:last] = (
+            next_grad[:, first:last].astype(jnp.float32) + scale * (slope - unit * projected)
+        ).astype(jnp.bfloat16)
+
+    for copy in ahead:
+        copy.wait_send()
+    for t in range(len(out_spans)):
+        sum_copy(t).wait_send()
 
     @pl.loop(1, count)
     def _(step):
@@ -317,22 +404,23 @@
                 line_copy(q, t).wait_send()
 
 
-def line_backward(normed, grads, weight_table, gate_up, down_proj):
+def line_backward(hidden, gains, grads, weight_table, gate_up, down_proj):
     count = weight_table.shape[0]
     chips = count // 2
-    rows, width = normed.shape
+    rows, width = hidden.shape[1:]
     half = down_proj.shape[0]
-    pieces = len(spans(width, 768))
+    pieces = len(spans(width, tile_width))
     dma = pltpu.SemaphoreType.DMA
     flops = 2 * count * rows * width * 5 * half
     return pl.pallas_call(
         functools.partial(block_kernel, chips),
-        out_shape=jax.ShapeDtypeStruct((rows, width), jnp.float32),
-        in_specs=[pl.BlockSpec(memory_space=pl.ANY)] * 5,
+        out_shape=jax.ShapeDtypeStruct((1, rows, width), jnp.bfloat16),
+        in_specs=[pl.BlockSpec(memory_space=pl.ANY)] * 6,
         out_specs=pl.BlockSpec(memory_space=pltpu.VMEM),
         scratch_shapes=[
             pltpu.VMEM((count, rows, width), jnp.bfloat16),
             pltpu.VMEM((count, rows, width), jnp.bfloat16),
+            pltpu.VMEM((1, width), jnp.float32),
             pltpu.VMEM((count, 1, rows), jnp.float32),
             pltpu.VMEM((count, 1, rows), jnp.float32),
             pltpu.VMEM((width, 2 * half), jnp.bfloat16),
@@ -342,7 +430,12 @@
             pltpu.VMEM((count, rows, width), jnp.bfloat16),
             pltpu.VMEM((chips, rows, width), jnp.bfloat16),
             pltpu.VMEM((2, chips, rows, width), jnp.bfloat16),
-            dma((5,)),
+            pltpu.VMEM((rows, width), jnp.bfloat16),
+            pltpu.VMEM((rows, width), jnp.bfloat16),
+            pltpu.VMEM((1, width), jnp.float32),
+            pltpu.VMEM((rows, width), jnp.bfloat16),
+            pltpu.VMEM((rows, 1), jnp.float32),
+            dma((6,)), dma((3,)), dma((3,)), dma((pieces,)), dma((pieces,)),
             dma((count,)), dma((count,)), dma((count,)), dma((count,)),
             dma((count,)), dma((count,)), dma((count,)), dma((count,)),
             dma((count,)), dma((count,)),
@@ -355,7 +448,7 @@
         cost_estimate=pl.CostEstimate(
             flops=flops, bytes_accessed=10 * half * width, transcendentals=0
         ),
-    )(normed, grads, weight_table, gate_up, down_proj)
+    )(hidden, gains, grads, weight_table, gate_up, down_proj)
 
 
 def expert_backward(rows_in, grad_rows, gate_up, down_proj):
@@ -426,24 +519,23 @@
     gate_up = w_gate_up[0, 0]
     down_proj = w_down[0, 0]
     experts = lax.axis_size("expert")
+    block = tokens.size * 2
+    held = gate_up.size * 2 + down_proj.size * 2 + (4 * experts + 11) * block
+    if experts % 2 == 0 and held < vmem_bytes:
+        chosen = routes[None, :, :] == jnp.arange(experts, dtype=jnp.int32)[:, None, None]
+        weight_table = jnp.sum(jnp.where(chosen, weights[None, :, :], 0.0), axis=-1)
+        return line_backward(
+            hidden_in, norm_gain, out_grad, weight_table[:, None, :], gate_up, down_proj
+        )
     input_single_precision = tokens.astype(jnp.float32)
     inverse_root_mean = lax.rsqrt(
         jnp.mean(input_single_precision * input_single_precision, axis=-1, keepdims=True) + norm_eps
     )
     normalized_input = input_single_precision * inverse_root_mean
     rescaled_input = (normalized_input * gain_vector_row[None, :]).astype(jnp.bfloat16)
-    block = tokens.size * 2
-    held = gate_up.size * 2 + down_proj.size * 2 + (4 * experts + 9) * block
-    if experts % 2 == 0 and held < vmem_bytes:
-        chosen = routes[None, :, :] == jnp.arange(experts, dtype=jnp.int32)[:, None, None]
-        weight_table = jnp.sum(jnp.where(chosen, weights[None, :, :], 0.0), axis=-1)
-        dnorm = line_backward(
-            rescaled_input, incoming_gradient, weight_table[:, None, :], gate_up, down_proj
-        )
-    else:
-        dnorm = slab_backward(
-            rescaled_input, incoming_gradient, routes, weights, gate_up, down_proj, experts
-        )
+    dnorm = slab_backward(
+        rescaled_input, incoming_gradient, routes, weights, gate_up, down_proj, experts
+    )
     normalized_input_gradient = dnorm * gain_vector_row[None, :]
     projected_rows = jnp.mean(normalized_input_gradient * normalized_input, axis=-1, keepdims=True)
     section_gradient = (

time: 180 us -> 169 us (0.939)
  waiting for transfers between devices: 11.9 us -> 0 us
  Pallas kernels: 157 us -> 161 us
  other arithmetic: 4.47 us -> 1.3 us
  local copies, waits for them, and re-layouts: 4 us -> 6.79 us
  starting transfers between devices: 2.49 us -> 0 us
    ppermute x1 -> x0, waiting for transfers between devices: 11.9 us -> none  [shifted(): return lax.ppermute(value, axis, pairs)]
    pallas_call x1, Pallas kernels: 157 us -> 161 us  [line_backward(): pl.pallas_call(functools.partial(block_kernel, chips), out_shape=jax.Shap...]
    ppermute x1 -> x0, starting transfers between devices: 2.49 us -> none  [shifted(): return lax.ppermute(value, axis, pairs)]
    pallas_call x0 -> x1, local copies, waits for them, and re-layouts: none -> 2.26 us  [line_backward(): pl.pallas_call(functools.partial(block_kernel, chips), out_shape=jax.Shap...]
    reduce_sum x2 -> x0, other arithmetic: 2.16 us -> none  [the longest x1 1.92 us: per_device(): jnp.mean(normalized_input_gradient * normalized_input, axis=-1, keepdims=...]
    unnamed x15 -> x2, local copies, waits for them, and re-layouts: 3.64 us -> 4.53 us
  transfers between devices with their start and end apart: 1 -> 0, of which waited for: 1 -> 0; matrix products, arithmetic and copies ran while one was open for 0% -> 0% of each run, Pallas kernels for 0% -> 0%
where the time goes in v2:
time: 169 us
  Pallas kernels  161 us (95%)
  local copies, waits for them, and re-layouts  6.79 us (4%)
    pallas_call x1, Pallas kernels, line_backward(): pl.pallas_call(functools.partial(block_kernel, chips), out_shape=jax.Shap...  161 us
    unnamed x2, local copies, waits for them, and re-layouts  4.53 us

profile of v2, /device:TPU:0, one launch (start us, length us, event | category | flops | bytes accessed | tf_op | source)
XLA Modules:
  0.0 169.2 jit_solution(11199776341271694737)
XLA Ops:
  0.0 1.3 select_reduce_fusion
  1.3 2.3 %copy.13.hidden_hbm = bf16[1,128,2880]{2,1,0:T(8,128)(2,1)} copy(bf16[1,128,2880]{1,2,0:T(8,128)(2,1)} %param.7) | data formatting | bytes 1474560 | tf_op args[0]
  3.6 2.3 %copy.14.grad_hbm = bf16[1,128,2880]{2,1,0:T(8,128)(2,1)} copy(bf16[1,128,2880]{1,2,0:T(8,128)(2,1)} %param.9) | data formatting | bytes 1474560 | tf_op args[2]
  5.8 161.1 %shard_map.73 = bf16[1,128,2880]{2,1,0:T(8,128)(2,1)} custom-call(bf16[1,128,2880]{2,1,0:T(8,128)(2,1)} %copy.13.hidden_hbm, f32[1,2880]{1,0:T(1,128)} %gain_hbm.1, bf16[1,128,2880]{2,1,0:T(8,128)(2,1)} %copy.14.grad_hbm, f32[8,1,128]{2,1,0:T(1,128)} %bitcast.5, bf16[2880,2880]{1,0:T(8,128)(2,1)} %bitcast.8, bf16[1440,2880]{1,0:T(8,128)(2,1)} %bitcast.9), custom_call_target="tpu_custom_call" | custom-call | flops 42467328000 | bytes 41472000 | tf_op jit(solution)/shard_map/pallas_call | solution.py:415
  167.0 2.3 %copy.15 = bf16[1,128,2880]{1,2,0:T(8,128)(2,1)} copy(bf16[1,128,2880]{2,1,0:T(8,128)(2,1)} %shard_map.73) | data formatting | bytes 1474560 | tf_op jit(solution)/shard_map/pallas_call | solution.py:415

commit v3 on v2

--- a/solution.py
+++ b/solution.py
@@ -40,14 +40,14 @@
     c = me % 2
     other = 1 - c
     count = 2 * chips
-    rows, width = hidden_hbm.shape[1:]
+    width, rows = hidden_hbm.shape[1:]
     half = down_hbm.shape[0]
     out_spans = spans(width, tile_width)
 
     def device(chip, core):
         return {"expert": 2 * chip + core}
 
-    load_x = pltpu.make_async_copy(hidden_hbm.at[0], xs.at[me], load_sems.at[0])
+    load_x = pltpu.make_async_copy(hidden_hbm.at[0], act.at[:, pl.ds(0, rows)], load_sems.at[0])
     load_g = pltpu.make_async_copy(grad_hbm.at[0], gs.at[me], load_sems.at[1])
     load_w = pltpu.make_async_copy(wtab_hbm, wtab, load_sems.at[2])
     load_gate_up = pltpu.make_async_copy(gate_up_hbm, gate_up, load_sems.at[3])
@@ -72,12 +72,14 @@
     load_x.wait()
     load_gain.wait()
 
-    @pl.loop(0, rows // 16)
-    def _(r):
-        part = pl.ds(r * 16, 16)
-        wide = xs[me, part, :].astype(jnp.float32)
-        scale = lax.rsqrt(jnp.mean(wide * wide, axis=-1, keepdims=True) + norm_eps)
-        xs[me, part, :] = (wide * scale * gain[...]).astype(jnp.bfloat16)
+    squares = jnp.zeros((1, rows), jnp.float32)
+    for first, last in spans(width, rows):
+        wide = act[first:last, 0:rows].astype(jnp.float32)
+        squares += jnp.sum(wide * wide, axis=0, keepdims=True)
+    own_scale = lax.rsqrt(squares / width + norm_eps)
+    for first, last in spans(width, rows):
+        unit = act[first:last, 0:rows].astype(jnp.float32) * own_scale
+        xs[me, :, first:last] = (unit.T * gain[:, first:last]).astype(jnp.bfloat16)
 
     pl.semaphore_wait(barrier, count + 1)
 
@@ -97,8 +99,8 @@
     def sum_copy(t):
         first, last = out_spans[t]
         return pltpu.make_async_remote_copy(
-            src_ref=res.at[me, :, pl.ds(first, last - first)],
-            dst_ref=next_sum.at[:, pl.ds(first, last - first)],
+            src_ref=res.at[me, pl.ds(first, last - first)],
+            dst_ref=next_sum.at[pl.ds(first, last - first)],
             send_sem=sum_send.at[t], recv_sem=sum_recv.at[t],
             device_id={"section": preceding},
         )
@@ -166,8 +168,8 @@
     def cross_copy(q, t):
         first, last = out_spans[t]
         return pltpu.make_async_remote_copy(
-            src_ref=res.at[2 * q + other, :, pl.ds(first, last - first)],
-            dst_ref=cross_in.at[q, :, pl.ds(first, last - first)],
+            src_ref=res.at[2 * q + other, pl.ds(first, last - first)],
+            dst_ref=cross_in.at[q, pl.ds(first, last - first)],
             send_sem=cross_send.at[q, t], recv_sem=cross_recv.at[q, t],
             device_id=device(p, other),
         )
@@ -180,8 +182,8 @@
         toward = jnp.where(q > p, jnp.minimum(p + 1, chips - 1), jnp.maximum(p - 1, 0))
         slot = jnp.where(q > p, 0, 1)
         return pltpu.make_async_remote_copy(
-            src_ref=res.at[2 * q + c, :, pl.ds(first, last - first)],
-            dst_ref=line_in.at[slot, q, :, pl.ds(first, last - first)],
+            src_ref=res.at[2 * q + c, pl.ds(first, last - first)],
+            dst_ref=line_in.at[slot, q, pl.ds(first, last - first)],
             send_sem=line_send.at[q, t], recv_sem=line_recv.at[slot, q, t],
             device_id=device(toward, c),
         )
@@ -189,8 +191,8 @@
     def line_arrival(slot, q, t):
         first, last = out_spans[t]
         return pltpu.make_async_remote_copy(
-            src_ref=res.at[2 * q + c, :, pl.ds(first, last - first)],
-            dst_ref=line_in.at[slot, q, :, pl.ds(first, last - first)],
+            src_ref=res.at[2 * q + c, pl.ds(first, last - first)],
+            dst_ref=line_in.at[slot, q, pl.ds(first, last - first)],
             send_sem=line_send.at[q, t], recv_sem=line_recv.at[slot, q, t],
             device_id=device(p, other),
         )
@@ -198,10 +200,10 @@
     def combine(q, t):
         first, last = out_spans[t]
         cross_arrival(q, t).wait_recv()
-        summed = res[2 * q + c, :, first:last].astype(jnp.float32) + cross_in[
-            q, :, first:last
+        summed = res[2 * q + c, first:last, :].astype(jnp.float32) + cross_in[
+            q, first:last, :
         ].astype(jnp.float32)
-        res[2 * q + c, :, first:last] = summed.astype(jnp.bfloat16)
+        res[2 * q + c, first:last, :] = summed.astype(jnp.bfloat16)
         starts = ((p == chips - 1) & (q < p)) | ((p == 0) & (q > p))
 
         @pl.when(starts)
@@ -232,40 +234,32 @@
         core_copy(xs, 2 * q + other, cr_x, recv_x).wait_recv()
         inputs = xs[pl.ds(2 * q, 2)].reshape(2 * rows, width)
         for first, last in spans(2 * half, 512):
-            pre[:, first:last] = jnp.dot(
+            pre[first:last, :] = jnp.dot(
                 inputs, gate_up[:, first:last], preferred_element_type=jnp.float32
-            )
+            ).T
 
     def backward_part(q):
         core_copy(gs, 2 * q + other, cr_g, recv_g).wait_recv()
-        diagonal = lax.broadcasted_iota(jnp.int32, (rows, rows), 0) == lax.broadcasted_iota(
-            jnp.int32, (rows, rows), 1
-        )
         for core in range(2):
-            across = jnp.broadcast_to(ws[2 * q + core], (rows, rows))
-            column = jnp.sum(jnp.where(diagonal, across, 0.0), axis=1, keepdims=True)
-            act[core * rows:(core + 1) * rows, :] = (
-                column * gs[2 * q + core].astype(jnp.float32)
+            act[:, core * rows:(core + 1) * rows] = (
+                ws[2 * q + core] * gs[2 * q + core].astype(jnp.float32)
             ).astype(jnp.bfloat16)
         for first, last in spans(half, 512):
-            dact = lax.dot_general(
-                act[...], down[first:last, :], (((1,), (1,)), ((), ())),
-                preferred_element_type=jnp.float32,
-            )
-            gate = pre[:, first:last]
-            up_part = pre[:, half + first:half + last]
+            dact = jnp.dot(down[first:last, :], act[...], preferred_element_type=jnp.float32)
+            gate = pre[first:last, :]
+            up_part = pre[half + first:half + last, :]
             sig = jax.nn.sigmoid(glu_alpha * gate)
-            pre[:, first:last] = dact * (up_part + 1.0) * (
+            pre[first:last, :] = dact * (up_part + 1.0) * (
                 sig + glu_alpha * gate * sig * (1.0 - sig)
             )
-            pre[:, half + first:half + last] = dact * gate * sig
+            pre[half + first:half + last, :] = dact * gate * sig
         act[...] = pre[...].astype(jnp.bfloat16)
         for t, (first, last) in enumerate(out_spans):
-            part = lax.dot_general(
-                act[...], gate_up[first:last, :], (((1,), (1,)), ((), ())),
-                preferred_element_type=jnp.float32,
+            part = jnp.dot(
+                gate_up[first:last, :], act[...], preferred_element_type=jnp.float32
             ).astype(jnp.bfloat16)
-            res[pl.ds(2 * q, 2), :, first:last] = part.reshape(2, rows, last - first)
+            for core in range(2):
+                res[2 * q + core, first:last, :] = part[:, core * rows:(core + 1) * rows]
             cross_copy(q, t).start()
             if t > 0:
                 combine(q, t - 1)
@@ -310,10 +304,10 @@
     def relay(slot, q, t):
         first, last = out_spans[t]
         line_arrival(slot, q, t).wait_recv()
-        summed = res[2 * q + c, :, first:last].astype(jnp.float32) + line_in[
-            slot, q, :, first:last
+        summed = res[2 * q + c, first:last, :].astype(jnp.float32) + line_in[
+            slot, q, first:last, :
         ].astype(jnp.float32)
-        res[2 * q + c, :, first:last] = summed.astype(jnp.bfloat16)
+        res[2 * q + c, first:last, :] = summed.astype(jnp.bfloat16)
         line_copy(q, t).start()
 
     inner = (p > 0) & (p < chips - 1)
@@ -335,11 +329,13 @@
     for copy in ahead:
         copy.wait_recv()
 
-    @pl.loop(0, rows // 16)
-    def _(r):
-        part = pl.ds(r * 16, 16)
-        wide = next_hidden[part, :].astype(jnp.float32)
-        inverse[part, :] = lax.rsqrt(jnp.mean(wide * wide, axis=-1, keepdims=True) + norm_eps)
+    squares = jnp.zeros((1, rows), jnp.float32)
+    for first, last in spans(width, rows):
+        wide = next_hidden[first:last, :].astype(jnp.float32)
+        squares += jnp.sum(wide * wide, axis=0, keepdims=True)
+        across = jnp.broadcast_to(next_gain[:, first:last], (rows, last - first))
+        pre[first:last, 0:rows] = across.T
+    inverse[...] = lax.rsqrt(squares / width + norm_eps)
 
     for t, (first, last) in enumerate(out_spans):
         for slot in range(2):
@@ -347,28 +343,29 @@
             def _(slot=slot, t=t, first=first, last=last):
                 line_arrival(slot, p, t).wait_recv()
 
-        below = jnp.where(p > 0, line_in[0, p, :, first:last].astype(jnp.float32), 0.0)
-        above = jnp.where(p < chips - 1, line_in[1, p, :, first:last].astype(jnp.float32), 0.0)
-        res[me, :, first:last] = (
-            res[me, :, first:last].astype(jnp.float32) + below + above
+        below = jnp.where(p > 0, line_in[0, p, first:last, :].astype(jnp.float32), 0.0)
+        above = jnp.where(p < chips - 1, line_in[1, p, first:last, :].astype(jnp.float32), 0.0)
+        res[me, first:last, :] = (
+            res[me, first:last, :].astype(jnp.float32) + below + above
         ).astype(jnp.bfloat16)
         sum_copy(t).start()
 
     relay_all(chips - 1)
 
     scale = inverse[...]
-    projected = jnp.zeros((rows, 1), jnp.float32)
+    projected = jnp.zeros((1, rows), jnp.float32)
     for t, (first, last) in enumerate(out_spans):
         sum_copy(t).wait_recv()
-        slope = next_sum[:, first:last].astype(jnp.float32) * next_gain[:, first:last]
-        unit = next_hidden[:, first:last].astype(jnp.float32) * scale
-        projected += jnp.sum(slope * unit, axis=1, keepdims=True)
+        slope = next_sum[first:last, :].astype(jnp.float32) * pre[first:last, 0:rows]
+        unit = next_hidden[first:last, :].astype(jnp.float32) * scale
+        pre[first:last, rows:2 * rows] = slope
+        projected += jnp.sum(slope * unit, axis=0, keepdims=True)
     projected = projected / width
     for first, last in out_spans:
-        slope = next_sum[:, first:last].astype(jnp.float32) * next_gain[:, first:last]
-        unit = next_hidden[:, first:last].astype(jnp.float32) * scale
-        out_ref[0, :, first:last] = (
-            next_grad[:, first:last].astype(jnp.float32) + scale * (slope - unit * projected)
+        unit = next_hidden[first:last, :].astype(jnp.float32) * scale
+        out_ref[0, first:last, :] = (
+            next_grad[first:last, :].astype(jnp.float32)
+            + scale * (pre[first:last, rows:2 * rows] - unit * projected)
         ).astype(jnp.bfloat16)
 
     for copy in ahead:
@@ -407,34 +404,34 @@
 def line_backward(hidden, gains, grads, weight_table, gate_up, down_proj):
     count = weight_table.shape[0]
     chips = count // 2
-    rows, width = hidden.shape[1:]
+    width, rows = hidden.shape[1:]
     half = down_proj.shape[0]
     pieces = len(spans(width, tile_width))
     dma = pltpu.SemaphoreType.DMA
     flops = 2 * count * rows * width * 5 * half
     return pl.pallas_call(
         functools.partial(block_kernel, chips),
-        out_shape=jax.ShapeDtypeStruct((1, rows, width), jnp.bfloat16),
+        out_shape=jax.ShapeDtypeStruct((1, width, rows), jnp.bfloat16),
         in_specs=[pl.BlockSpec(memory_space=pl.ANY)] * 6,
         out_specs=pl.BlockSpec(memory_space=pltpu.VMEM),
         scratch_shapes=[
             pltpu.VMEM((count, rows, width), jnp.bfloat16),
-            pltpu.VMEM((count, rows, width), jnp.bfloat16),
+            pltpu.VMEM((count, width, rows), jnp.bfloat16),
             pltpu.VMEM((1, width), jnp.float32),
             pltpu.VMEM((count, 1, rows), jnp.float32),
             pltpu.VMEM((count, 1, rows), jnp.float32),
             pltpu.VMEM((width, 2 * half), jnp.bfloat16),
             pltpu.VMEM((half, width), jnp.bfloat16),
-            pltpu.VMEM((2 * rows, 2 * half), jnp.float32),
-            pltpu.VMEM((2 * rows, width), jnp.bfloat16),
-            pltpu.VMEM((count, rows, width), jnp.bfloat16),
-            pltpu.VMEM((chips, rows, width), jnp.bfloat16),
-            pltpu.VMEM((2, chips, rows, width), jnp.bfloat16),
-            pltpu.VMEM((rows, width), jnp.bfloat16),
-            pltpu.VMEM((rows, width), jnp.bfloat16),
+            pltpu.VMEM((max(width, 2 * half), 2 * rows), jnp.float32),
+            pltpu.VMEM((width, 2 * rows), jnp.bfloat16),
+            pltpu.VMEM((count, width, rows), jnp.bfloat16),
+            pltpu.VMEM((chips, width, rows), jnp.bfloat16),
+            pltpu.VMEM((2, chips, width, rows), jnp.bfloat16),
+            pltpu.VMEM((width, rows), jnp.bfloat16),
+            pltpu.VMEM((width, rows), jnp.bfloat16),
             pltpu.VMEM((1, width), jnp.float32),
-            pltpu.VMEM((rows, width), jnp.bfloat16),
-            pltpu.VMEM((rows, 1), jnp.float32),
+            pltpu.VMEM((width, rows), jnp.bfloat16),
+            pltpu.VMEM((1, rows), jnp.float32),
             dma((6,)), dma((3,)), dma((3,)), dma((pieces,)), dma((pieces,)),
             dma((count,)), dma((count,)), dma((count,)), dma((count,)),
             dma((count,)), dma((count,)), dma((count,)), dma((count,)),
@@ -524,9 +521,11 @@
     if experts % 2 == 0 and held < vmem_bytes:
         chosen = routes[None, :, :] == jnp.arange(experts, dtype=jnp.int32)[:, None, None]
         weight_table = jnp.sum(jnp.where(chosen, weights[None, :, :], 0.0), axis=-1)
-        return line_backward(
-            hidden_in, norm_gain, out_grad, weight_table[:, None, :], gate_up, down_proj
-        )
+        result = line_backward(
+            hidden_in.transpose(0, 2, 1), norm_gain, out_grad.transpose(0, 2, 1),
+            weight_table[:, None, :], gate_up, down_proj,
+        )
+        return result.transpose(0, 2, 1)
     input_single_precision = tokens.astype(jnp.float32)
     inverse_root_mean = lax.rsqrt(
         jnp.mean(input_single_precision * input_single_precision, axis=-1, keepdims=True) + norm_eps

time: 169 us -> 169 us (level)
  Pallas kernels: 161 us -> 166 us
  local copies, waits for them, and re-layouts: 6.79 us -> 2.03 us
    pallas_call x1, Pallas kernels: 161 us -> 166 us  [line_backward(): pl.pallas_call(functools.partial(block_kernel, chips), out_shape=jax.Shap...]
    unnamed x2 -> x1, local copies, waits for them, and re-layouts: 4.53 us -> 2.03 us
    pallas_call x1 -> x0, local copies, waits for them, and re-layouts: 2.26 us -> none  [line_backward(): pl.pallas_call(functools.partial(block_kernel, chips), out_shape=jax.Shap...]
where the time goes in v3:
time: 169 us
  Pallas kernels  166 us (98%)
  local copies, waits for them, and re-layouts  2.03 us (1%)
    pallas_call x1, Pallas kernels, line_backward(): pl.pallas_call(functools.partial(block_kernel, chips), out_shape=jax.Shap...  166 us

profile of v3, /device:TPU:0, one launch (start us, length us, event | category | flops | bytes accessed | tf_op | source)
XLA Modules:
  0.0 169.0 jit_solution(11402429690122009786)
XLA Ops:
  0.0 1.3 select_reduce_fusion
  1.3 165.7 %shard_map.73 = bf16[1,2880,128]{2,1,0:T(8,128)(2,1)} custom-call(bf16[1,2880,128]{2,1,0:T(8,128)(2,1)} %bitcast.14, f32[1,2880]{1,0:T(1,128)} %gain_hbm.1, bf16[1,2880,128]{2,1,0:T(8,128)(2,1)} %bitcast.15, f32[8,1,128]{2,1,0:T(1,128)} %bitcast.9, bf16[2880,2880]{1,0:T(8,128)(2,1)} %bitcast.12, bf16[1440,2880]{1,0:T(8,128)(2,1)} %bitcast.13), custom_call_target="tpu_custom_call" | custom-call | flops 42467328000 | bytes 41472000 | tf_op jit(solution)/shard_map/pallas_call | solution.py:412
  167.0 2.0 %copy.11 = bf16[1,128,2880]{1,2,0:T(8,128)(2,1)} copy(bf16[1,128,2880]{1,2,0:T(8,128)(2,1)} %bitcast.8) | data formatting | bytes 1474560

commit v4 on v3

--- a/solution.py
+++ b/solution.py
@@ -135,12 +135,15 @@
     def core_copy(buf, slot, send, recv):
         return gather_copy(buf, slot, send, recv, p, other)
 
-    def send_own(buf, up_sem, dn_sem, recv):
-        @pl.when(p < chips - 1)
+    last_chip = chips - 1
+    inner = (p > 0) & (p < last_chip)
+
+    def send_own(buf, up_sem, dn_sem, recv, up_now, down_now):
+        @pl.when((p < last_chip) & up_now)
         def _():
             up_copy(buf, me, up_sem, recv).start()
 
-        @pl.when(p > 0)
+        @pl.when((p > 0) & down_now)
         def _():
             down_copy(buf, me, dn_sem, recv).start()
 
@@ -211,7 +214,7 @@
             line_copy(q, t).start()
 
     core_copy(xs, me, cr_x, recv_x).start()
-    send_own(xs, up_x, dn_x, recv_x)
+    send_own(xs, up_x, dn_x, recv_x, p >= 0, p >= 0)
     load_g.wait()
     core_copy(gs, me, cr_g, recv_g).start()
     for copy in ahead:
@@ -266,40 +269,57 @@
         combine(q, len(out_spans) - 1)
 
     low = p < chips // 2
-
-    def chunk_of(k, first_turn):
-        return jnp.where(low == first_turn, p + k, p - k)
-
-    def inside(q):
-        return (q >= 0) & (q < chips)
-
-    @pl.loop(0, 2 * chips - 1)
+    up_late = p == last_chip - 1
+    down_late = p == 1
+
+    def pass_x(k):
+        pass_on(k, xs, up_x, dn_x, cr_x, recv_x)
+
+    def pass_g(k):
+        pass_on(k, gs, up_g, dn_g, cr_g, recv_g)
+
+    def turn_value(i, values):
+        chosen = values[-1]
+        for number in range(len(values) - 2, -1, -1):
+            chosen = jnp.where(i == number, values[number], chosen)
+        return chosen
+
+    @pl.loop(0, chips)
     def _(i):
-        k = (i + 1) // 2
-        leading = i % 2 == 1
-        q = chunk_of(k, leading)
-        valid = inside(q)
-        paired = inside(chunk_of(k - 1, False)) & (k >= 2)
-
-        @pl.when(valid)
-        def _():
-            forward_part(q)
-
-        @pl.when((leading & jnp.logical_not(paired)) | (jnp.logical_not(leading) & valid & (i > 0)))
-        def _():
-            pass_on(jnp.where(leading, k, k + 1), gs, up_g, dn_g, cr_g, recv_g)
+        offset = jnp.where(
+            inner, turn_value(i, (0, 1, -1, 2)), turn_value(i, (0, 2, 3, 1))
+        )
+        q = jnp.where(low, p + offset, p - offset)
+
+        @pl.when(jnp.logical_not(inner) & ((i == 1) | (i == 2)))
+        def _():
+            pass_x(i + 1)
+
+        forward_part(q)
 
         @pl.when(i == 0)
         def _():
-            send_own(gs, up_g, dn_g, recv_g)
-
-        @pl.when(valid)
-        def _():
-            backward_part(q)
-
-        @pl.when(leading | (i == 0))
-        def _():
-            pass_on(k + 1, xs, up_x, dn_x, cr_x, recv_x)
+            send_own(
+                gs, up_g, dn_g, recv_g, jnp.logical_not(up_late), jnp.logical_not(down_late)
+            )
+
+        @pl.when((i == 0) | (inner & (i == 1)))
+        def _():
+            pass_x(i + 1)
+
+        @pl.when(jnp.logical_not(inner) & (i > 0))
+        def _():
+            pass_g(turn_value(i, (0, 2, 3, 1)))
+
+        backward_part(q)
+
+        @pl.when(inner & (i < 2))
+        def _():
+            pass_g(i + 1)
+
+        @pl.when(i == 1)
+        def _():
+            send_own(gs, up_g, dn_g, recv_g, up_late, down_late)
 
     def relay(slot, q, t):
         first, last = out_spans[t]
@@ -310,8 +330,6 @@
         res[2 * q + c, first:last, :] = summed.astype(jnp.bfloat16)
         line_copy(q, t).start()
 
-    inner = (p > 0) & (p < chips - 1)
-
     def relay_all(distance):
         for t in range(len(out_spans)):
             for turn in range(2):
@@ -323,7 +341,7 @@
                 def _(slot=slot, q=q, t=t):
                     relay(slot, q, t)
 
-    for distance in range(1, chips - 1):
+    for distance in range(1, chips):
         relay_all(distance)
 
     for copy in ahead:
@@ -349,8 +367,6 @@
             res[me, first:last, :].astype(jnp.float32) + below + above
         ).astype(jnp.bfloat16)
         sum_copy(t).start()
-
-    relay_all(chips - 1)
 
     scale = inverse[...]
     projected = jnp.zeros((1, rows), jnp.float32)
@@ -518,7 +534,7 @@
     experts = lax.axis_size("expert")
     block = tokens.size * 2
     held = gate_up.size * 2 + down_proj.size * 2 + (4 * experts + 11) * block
-    if experts % 2 == 0 and held < vmem_bytes:
+    if experts == 8 and held < vmem_bytes:
         chosen = routes[None, :, :] == jnp.arange(experts, dtype=jnp.int32)[:, None, None]
         weight_table = jnp.sum(jnp.where(chosen, weights[None, :, :], 0.0), axis=-1)
         result = line_backward(

time: 169 us -> 178 us (1.053)
  the two profiles are of different devices: /device:TPU:0 before, /device:TPU:16 now
where the time goes in v4:
time: 178 us
  Pallas kernels  174 us (98%)
  local copies, waits for them, and re-layouts  2.03 us (1%)
    pallas_call x1, Pallas kernels, line_backward(): pl.pallas_call(functools.partial(block_kernel, chips), out_shape=jax.Shap...  174 us

profile of v4, /device:TPU:16, one launch (start us, length us, event | category | flops | bytes accessed | tf_op | source)
XLA Modules:
  0.0 177.7 jit_solution(15018743097404021587)
XLA Ops:
  0.0 1.3 select_reduce_fusion
  1.3 174.3 %shard_map.73 = bf16[1,2880,128]{2,1,0:T(8,128)(2,1)} custom-call(bf16[1,2880,128]{2,1,0:T(8,128)(2,1)} %bitcast.14, f32[1,2880]{1,0:T(1,128)} %gain_hbm.1, bf16[1,2880,128]{2,1,0:T(8,128)(2,1)} %bitcast.15, f32[8,1,128]{2,1,0:T(1,128)} %bitcast.9, bf16[2880,2880]{1,0:T(8,128)(2,1)} %bitcast.12, bf16[1440,2880]{1,0:T(8,128)(2,1)} %bitcast.13), custom_call_target="tpu_custom_call" | custom-call | flops 42467328000 | bytes 41472000 | tf_op jit(solution)/shard_map/pallas_call | solution.py:428
  175.6 2.0 %copy.11 = bf16[1,128,2880]{1,2,0:T(8,128)(2,1)} copy(bf16[1,128,2880]{1,2,0:T(8,128)(2,1)} %bitcast.8) | data formatting | bytes 1474560

commit v5 on v4

--- a/solution.py
+++ b/solution.py
@@ -138,12 +138,12 @@
     last_chip = chips - 1
     inner = (p > 0) & (p < last_chip)
 
-    def send_own(buf, up_sem, dn_sem, recv, up_now, down_now):
-        @pl.when((p < last_chip) & up_now)
+    def send_own(buf, up_sem, dn_sem, recv):
+        @pl.when(p < last_chip)
         def _():
             up_copy(buf, me, up_sem, recv).start()
 
-        @pl.when((p > 0) & down_now)
+        @pl.when(p > 0)
         def _():
             down_copy(buf, me, dn_sem, recv).start()
 
@@ -214,9 +214,10 @@
             line_copy(q, t).start()
 
     core_copy(xs, me, cr_x, recv_x).start()
-    send_own(xs, up_x, dn_x, recv_x, p >= 0, p >= 0)
+    send_own(xs, up_x, dn_x, recv_x)
     load_g.wait()
     core_copy(gs, me, cr_g, recv_g).start()
+    send_own(gs, up_g, dn_g, recv_g)
     for copy in ahead:
         copy.start()
     load_w.wait()
@@ -269,8 +270,6 @@
         combine(q, len(out_spans) - 1)
 
     low = p < chips // 2
-    up_late = p == last_chip - 1
-    down_late = p == 1
 
     def pass_x(k):
         pass_on(k, xs, up_x, dn_x, cr_x, recv_x)
@@ -287,39 +286,29 @@
     @pl.loop(0, chips)
     def _(i):
         offset = jnp.where(
-            inner, turn_value(i, (0, 1, -1, 2)), turn_value(i, (0, 2, 3, 1))
+            inner, turn_value(i, (0, 1, -1, 2)), i
         )
         q = jnp.where(low, p + offset, p - offset)
 
-        @pl.when(jnp.logical_not(inner) & ((i == 1) | (i == 2)))
+        @pl.when(jnp.logical_not(inner) & (i > 1))
+        def _():
+            pass_x(i)
+
+        forward_part(q)
+
+        @pl.when((i == 0) | (inner & (i == 1)))
         def _():
             pass_x(i + 1)
 
-        forward_part(q)
-
-        @pl.when(i == 0)
-        def _():
-            send_own(
-                gs, up_g, dn_g, recv_g, jnp.logical_not(up_late), jnp.logical_not(down_late)
-            )
-
-        @pl.when((i == 0) | (inner & (i == 1)))
-        def _():
-            pass_x(i + 1)
-
         @pl.when(jnp.logical_not(inner) & (i > 0))
         def _():
-            pass_g(turn_value(i, (0, 2, 3, 1)))
+            pass_g(i)
 
         backward_part(q)
 
         @pl.when(inner & (i < 2))
         def _():
             pass_g(i + 1)
-
-        @pl.when(i == 1)
-        def _():
-            send_own(gs, up_g, dn_g, recv_g, up_late, down_late)
 
     def relay(slot, q, t):
         first, last = out_spans[t]
@@ -341,7 +330,7 @@
                 def _(slot=slot, q=q, t=t):
                     relay(slot, q, t)
 
-    for distance in range(1, chips):
+    for distance in range(1, chips - 1):
         relay_all(distance)
 
     for copy in ahead:
@@ -367,6 +356,8 @@
             res[me, first:last, :].astype(jnp.float32) + below + above
         ).astype(jnp.bfloat16)
         sum_copy(t).start()
+
+    relay_all(chips - 1)
 
     scale = inverse[...]
     projected = jnp.zeros((1, rows), jnp.float32)

time: 178 us -> 174 us (0.978)
  the two profiles are of different devices: /device:TPU:16 before, /device:TPU:0 now
where the time goes in v5:
time: 174 us
  Pallas kernels  171 us (98%)
  local copies, waits for them, and re-layouts  2.03 us (1%)
    pallas_call x1, Pallas kernels, line_backward(): pl.pallas_call(functools.partial(block_kernel, chips), out_shape=jax.Shap...  171 us

profile of v5, /device:TPU:0, one launch (start us, length us, event | category | flops | bytes accessed | tf_op | source)
XLA Modules:
  0.0 174.2 jit_solution(11668275749818898959)
XLA Ops:
  0.0 1.3 select_reduce_fusion
  1.3 170.9 %shard_map.73 = bf16[1,2880,128]{2,1,0:T(8,128)(2,1)} custom-call(bf16[1,2880,128]{2,1,0:T(8,128)(2,1)} %bitcast.14, f32[1,2880]{1,0:T(1,128)} %gain_hbm.1, bf16[1,2880,128]{2,1,0:T(8,128)(2,1)} %bitcast.15, f32[8,1,128]{2,1,0:T(1,128)} %bitcast.9, bf16[2880,2880]{1,0:T(8,128)(2,1)} %bitcast.12, bf16[1440,2880]{1,0:T(8,128)(2,1)} %bitcast.13), custom_call_target="tpu_custom_call" | custom-call | flops 42467328000 | bytes 41472000 | tf_op jit(solution)/shard_map/pallas_call | solution.py:419
  172.2 2.0 %copy.11 = bf16[1,128,2880]{1,2,0:T(8,128)(2,1)} copy(bf16[1,128,2880]{1,2,0:T(8,128)(2,1)} %bitcast.8) | data formatting | bytes 1474560
